TPU v7x, 32 devices: a whole 2x2x4 slice. The times are simulated.
32 devices in a mesh: groups: 2 (over x), span: 16 (over z, y, core).
Axes of the slice: x: 2, y: 2, z: 4, core: 2. Of those that a mesh axis runs over, the one named last changes fastest.
Arguments:
- queries: bfloat16 [8192, 2560], P(('groups', 'span')), parts along dimension 0, may hold values from -100 to 100
- cross_queries: bfloat16 [8192, 2560], P(('groups', 'span')), parts along dimension 0, may hold values from -100 to 100
- frame_kv: bfloat16 [8192, 5120], P(('groups', 'span')), parts along dimension 0, may hold values from -7 to 7
- sink_kv: bfloat16 [32, 64, 5120], P(('groups', 'span')), parts along dimension 0, may hold values from -5 to 5
- prompt_kv: bfloat16 [4, 512, 5120], P('groups', 'span'), parts along dimension 0, may hold values from -7 to 7
- switch: int32 [8], P('groups'), parts along dimension 0, may hold values from 0 to 4
Outputs:
- self_out: bfloat16 [8192, 2560], P(('groups', 'span')), parts along dimension 0
- cross_out: bfloat16 [8192, 2560], P(('groups', 'span')), parts along dimension 0
There are 2 independent parts, one for each index of `groups`. A program takes and returns all parts, laid end to end along the dimension named above; each array names one. Nothing has to cross between parts.
All inputs are finite; a program needn't handle non-finite values.
Results may differ from a plain program's by a relative error of at most 0.006.
Values may be sent and summed in bfloat16 or wider, within the bound.
No kernel may reach another device: no remote copies, remote signals or barrier semaphores. Data moves between devices by JAX's collectives and lax.ppermute only.
A program may use at most 128 MiB of HBM per device.

v0:
```python
import math

import jax
import jax.numpy as jnp
from jax import lax
from jax.sharding import PartitionSpec as P

HEADS = 20
HDIM = 128
WIN = 4


def passed_along(value, axis, steps):
    count = lax.axis_size(axis)
    pairs = [(source, (source + steps) % count) for source in range(count)]
    return lax.ppermute(value, axis, pairs)


def blend_heads(query_rows, key_rows, usable):
    rows_here = query_rows.shape[0]
    key_count = key_rows.shape[0]
    width = HEADS * HDIM
    bundle = 4
    scaling = 1.0 / math.sqrt(HDIM)
    blended_parts = []
    for leading in range(0, HEADS, bundle):
        low = leading * HDIM
        high = (leading + bundle) * HDIM
        query_block = query_rows[:, low:high].reshape(rows_here, bundle, HDIM)
        key_block = key_rows[:, low:high].reshape(key_count, bundle, HDIM)
        value_block = key_rows[:, width + low : width + high].reshape(key_count, bundle, HDIM)
        scores = (
            jnp.einsum("qhd,khd->hqk", query_block, key_block, preferred_element_type=jnp.float32)
            * scaling
        )
        scores = jnp.where(usable[None, None, :], scores, -jnp.inf)
        row_max = jnp.max(scores, axis=-1, keepdims=True)
        weights = jnp.exp(scores - row_max)
        totals = jnp.sum(weights, axis=-1)
        blended = jnp.einsum(
            "hqk,khd->qhd",
            weights.astype(jnp.bfloat16),
            value_block,
            preferred_element_type=jnp.float32,
        )
        blended = blended / jnp.transpose(totals)[:, :, None]
        blended_parts.append(blended.astype(jnp.bfloat16).reshape(rows_here, bundle * HDIM))
    return jnp.concatenate(blended_parts, axis=1)


def shards(queries, cross_queries, frame_kv, sink_kv, prompt_kv, switch):
    stream_count = lax.axis_size("span") // WIN
    device = lax.axis_index("span")
    place = device // stream_count
    stream_of = device % stream_count
    stream_ids = jnp.arange(switch.shape[0], dtype=jnp.int32)
    switch_at = jnp.sum(jnp.where(stream_ids == stream_of, switch, 0))
    prompt_pick = (place >= switch_at).astype(jnp.int32)
    rows_here = queries.shape[0]
    width = HEADS * HDIM
    own_sink = sink_kv.reshape(sink_kv.shape[1], sink_kv.shape[2])
    frame_parts = [frame_kv]
    frame_flags = [jnp.array(True)]
    sink_parts = [own_sink]
    carried_frame = frame_kv
    carried_sink = own_sink
    for offset in range(1, WIN):
        carried_frame, carried_sink = passed_along(
            (carried_frame, carried_sink), "span", stream_count
        )
        frame_parts.append(carried_frame)
        frame_flags.append(place >= offset)
        sink_parts.append(carried_sink)
    sink_rows = jnp.concatenate(sink_parts, axis=0)
    key_rows = jnp.concatenate([sink_rows] + frame_parts, axis=0)
    usable = jnp.concatenate(
        [jnp.ones((sink_rows.shape[0],), jnp.bool_)]
        + [
            jnp.broadcast_to(flag, (piece.shape[0],))
            for piece, flag in zip(frame_parts, frame_flags)
        ]
    )
    self_out = blend_heads(queries, key_rows, usable)
    query_heads = cross_queries.reshape(rows_here, HEADS, HDIM)
    scaling = 1.0 / math.sqrt(HDIM)
    maxima = jnp.full((HEADS, rows_here), -jnp.inf, jnp.float32)
    sums = jnp.zeros((HEADS, rows_here), jnp.float32)
    accum = jnp.zeros((rows_here, HEADS, HDIM), jnp.float32)
    picked = lax.dynamic_index_in_dim(
        lax.all_gather(prompt_kv, "span", axis=1, tiled=True), prompt_pick, 0, keepdims=False
    )
    piece_rows = picked.shape[0]
    key_heads = picked[:, :width].reshape(piece_rows, HEADS, HDIM)
    value_heads = picked[:, width:].reshape(piece_rows, HEADS, HDIM)
    scores = (
        jnp.einsum("qhd,khd->hqk", query_heads, key_heads, preferred_element_type=jnp.float32)
        * scaling
    )
    new_max = jnp.max(scores, axis=-1)
    rescale = jnp.exp(maxima - new_max)
    weights = jnp.exp(scores - new_max[:, :, None])
    sums = sums * rescale + jnp.sum(weights, axis=-1)
    added = jnp.einsum(
        "hqk,khd->qhd",
        weights.astype(jnp.bfloat16),
        value_heads,
        preferred_element_type=jnp.float32,
    )
    accum = accum * jnp.transpose(rescale)[:, :, None] + added
    maxima, sums, accum = (new_max, sums, accum)
    cross_out = (
        (accum / jnp.transpose(sums)[:, :, None]).astype(jnp.bfloat16).reshape(rows_here, width)
    )
    return (self_out, cross_out)


def solution(mesh):
    in_specs = (
        P(("groups", "span"), None),
        P(("groups", "span"), None),
        P(("groups", "span"), None),
        P(("groups", "span"), None, None),
        P("groups", "span", None),
        P("groups"),
    )
    out_specs = (P(("groups", "span"), None), P(("groups", "span"), None))
    return jax.shard_map(shards, mesh=mesh, in_specs=in_specs, out_specs=out_specs, check_vma=False)
```

profile of v0, /device:TPU:0, one launch (start us, length us, event | category | flops | bytes accessed | tf_op | source)
XLA Modules:
  0.0 389.2 jit_solution(17533499278320517781)
XLA Ops:
  7.9 3.0 copy.67
  11.0 3.1 collective-permute-start.3
  14.0 98.6 %collective-permute-done.3 = bf16[256,5120]{0,1:T(8,128)(2,1)S(1)} collective-permute-done((bf16[256,5120]{0,1:T(8,128)(2,1)S(1)}, bf16[256,5120]{0,1:T(8,128)(2,1)S(1)}, u32[]{:S(2)}, u32[]{:S(2)}) %collective-permute-start.3) | collective-permute-done | bytes 2621472 | tf_op jit(solution)/shard_map/ppermute | solution.py:16
  114.2 19.7 %collective-permute-start.4 = (bf16[256,5120]{0,1:T(8,128)(2,1)S(1)}, bf16[256,5120]{0,1:T(8,128)(2,1)}, u32[]{:S(2)}, u32[]{:S(2)}) collective-permute-start(bf16[256,5120]{0,1:T(8,128)(2,1)S(1)} %collective-permute-done.3), channel_id=1, source_target_pairs={{0,4},{1,5},{2,6},{3,7},{4,8},{5,9},{6,10},{7,11},{8,12},{9,13},{1... | collective-permute-start | bytes 7864328 | tf_op jit(solution)/shard_map/ppermute | solution.py:16
  133.9 58.9 %collective-permute-done.4 = bf16[256,5120]{0,1:T(8,128)(2,1)} collective-permute-done((bf16[256,5120]{0,1:T(8,128)(2,1)S(1)}, bf16[256,5120]{0,1:T(8,128)(2,1)}, u32[]{:S(2)}, u32[]{:S(2)}) %collective-permute-start.4) | collective-permute-done | bytes 2621472 | tf_op jit(solution)/shard_map/ppermute | solution.py:16
  193.7 70.7 %collective-permute-done = bf16[64,5120]{1,0:T(8,128)(2,1)S(1)} collective-permute-done((bf16[64,5120]{1,0:T(8,128)(2,1)S(1)}, bf16[64,5120]{1,0:T(8,128)(2,1)S(1)}, u32[]{:S(2)}, u32[]{:S(2)}) %collective-permute-start) | collective-permute-done | bytes 655392 | tf_op jit(solution)/shard_map/ppermute | solution.py:16
  265.2 14.7 %collective-permute-done.1 = bf16[64,5120]{1,0:T(8,128)(2,1)} collective-permute-done((bf16[64,5120]{1,0:T(8,128)(2,1)S(1)}, bf16[64,5120]{1,0:T(8,128)(2,1)}, u32[]{:S(2)}, u32[]{:S(2)}) %collective-permute-start.1) | collective-permute-done | bytes 655392 | tf_op jit(solution)/shard_map/ppermute | solution.py:16
  282.6 2.2 fusion.90
  288.8 2.4 copy.94
  291.3 2.3 copy.64
  293.6 2.3 copy.65
  295.9 2.3 copy.66
  298.2 20.5 %concatenate.12 = bf16[1280,5120]{0,1:T(8,128)(2,1)} concatenate(bf16[64,5120]{0,1:T(8,128)(2,1)} %bitcast.186, bf16[64,5120]{0,1:T(8,128)(2,1)} %copy.64, bf16[64,5120]{0,1:T(8,128)(2,1)} %copy.65, bf16[64,5120]{0,1:T(8,128)(2,1)} %copy.66, bf16[256,5120]{0,1:T(8,128)(2,1)S(1)} %copy.67, bf16[256,5120]{0,1:T(8,128)(2,1)} %copy-done.3, bf16[256,5120]{0,1:T(8,128)(2,1)} %collective-permute-done.4, ...), dimensions={0} | concatenate | bytes 26214400 | tf_op jit(solution)/shard_map/concatenate | solution.py:75
  318.7 8.1 %fusion.88 = (bf16[1280,512]{0,1:T(8,128)(2,1)S(1)}, bf16[1280,512]{0,1:T(8,128)(2,1)S(1)}, bf16[1280,512]{0,1:T(8,128)(2,1)}, bf16[1280,512]{0,1:T(8,128)(2,1)}...) fusion(bf16[1280,5120]{0,1:T(8,128)(2,1)} %concatenate.12), kind=kLoop, calls=%fused_computation.78 | loop fusion | bytes 26214400 | tf_op jit(solution)/shard_map/slice | solution.py:30
  332.9 2.6 bitcast_reduce_fusion.4
  340.4 2.6 bitcast_reduce_fusion.3
  347.1 2.6 bitcast_reduce_fusion.2
  353.8 1.9 bitcast_reduce_fusion.1
  361.2 2.8 dynamic-slice_bitcast_fusion
  364.1 1.9 fusion.89
  366.0 4.4 %copy.97 = bf16[512,2560]{0,1:T(8,128)(2,1)} copy(bf16[512,2560]{1,0:T(8,128)(2,1)} %get-tuple-element.19) | data formatting | bytes 5242880 | tf_op jit(solution)/shard_map/slice | solution.py:94
  370.4 2.6 copy.93
  373.0 3.7 bitcast_reduce_fusion
  378.5 2.3 fusion.33
  (68 shorter events, 38.1 us)
Async XLA Ops:
  7.2 354.1 %all-gather.2.cloned.1.call-start = ((), (), s32[]{:S(2)}) async-start(), calls=%async_computation | async-start | bytes 11141120 | tf_op jit(solution)/shard_map/all_gather | solution.py:90
  7.9 184.9 %copy-start.8 = (bf16[1,64,5120]{2,1,0:T(8,128)(2,1)S(1)}, bf16[1,64,5120]{2,1,0:T(8,128)(2,1)}, u32[]{:S(2)}) copy-start(bf16[1,64,5120]{2,1,0:T(8,128)(2,1)} %param.9) | copy-start | bytes 1966084
  7.9 273.4 %copy-start.10 = (s32[4]{0:T(128)S(1)}, s32[4]{0:T(128)}, u32[]{:S(2)}) copy-start(s32[4]{0:T(128)} %param.11) | copy-start | bytes 52
  11.0 101.7 %collective-permute-start.3 = (bf16[256,5120]{0,1:T(8,128)(2,1)S(1)}, bf16[256,5120]{0,1:T(8,128)(2,1)S(1)}, u32[]{:S(2)}, u32[]{:S(2)}) collective-permute-start(bf16[256,5120]{0,1:T(8,128)(2,1)S(1)} %copy.67), channel_id=1, source_target_pairs={{0,4},{1,5},{2,6},{3,7},{4,8},{5,9},{6,10},{7,11},{8,12},{9,13},{1... | collective-permute-start | bytes 7864328 | tf_op jit(solution)/shard_map/ppermute | solution.py:16
  112.6 1.5 copy-start.3
  114.2 78.6 %collective-permute-start.4 = (bf16[256,5120]{0,1:T(8,128)(2,1)S(1)}, bf16[256,5120]{0,1:T(8,128)(2,1)}, u32[]{:S(2)}, u32[]{:S(2)}) collective-permute-start(bf16[256,5120]{0,1:T(8,128)(2,1)S(1)} %collective-permute-done.3), channel_id=1, source_target_pairs={{0,4},{1,5},{2,6},{3,7},{4,8},{5,9},{6,10},{7,11},{8,12},{9,13},{1... | collective-permute-start | bytes 7864328 | tf_op jit(solution)/shard_map/ppermute | solution.py:16
  192.8 105.5 %collective-permute-start.5 = (bf16[256,5120]{0,1:T(8,128)(2,1)}, bf16[256,5120]{0,1:T(8,128)(2,1)}, u32[]{:S(2)}, u32[]{:S(2)}) collective-permute-start(bf16[256,5120]{0,1:T(8,128)(2,1)} %collective-permute-done.4), channel_id=1, source_target_pairs={{0,4},{1,5},{2,6},{3,7},{4,8},{5,9},{6,10},{7,11},{8,12},{9,13},{1... | collective-permute-start | bytes 7864328 | tf_op jit(solution)/shard_map/ppermute | solution.py:16
  192.8 71.6 %collective-permute-start = (bf16[64,5120]{1,0:T(8,128)(2,1)S(1)}, bf16[64,5120]{1,0:T(8,128)(2,1)S(1)}, u32[]{:S(2)}, u32[]{:S(2)}) collective-permute-start(bf16[64,5120]{1,0:T(8,128)(2,1)S(1)} %bitcast.210), channel_id=1, source_target_pairs={{0,4},{1,5},{2,6},{3,7},{4,8},{5,9},{6,10},{7,11},{8,12},{9,13},{1... | collective-permute-start | bytes 1966088 | tf_op jit(solution)/shard_map/ppermute | solution.py:16
  264.4 0.9 copy-start.9
  265.2 14.7 %collective-permute-start.1 = (bf16[64,5120]{1,0:T(8,128)(2,1)S(1)}, bf16[64,5120]{1,0:T(8,128)(2,1)}, u32[]{:S(2)}, u32[]{:S(2)}) collective-permute-start(bf16[64,5120]{1,0:T(8,128)(2,1)S(1)} %collective-permute-done), channel_id=1, source_target_pairs={{0,4},{1,5},{2,6},{3,7},{4,8},{5,9},{6,10},{7,11},{8,12},{9,13},{1... | collective-permute-start | bytes 1966088 | tf_op jit(solution)/shard_map/ppermute | solution.py:16
  279.9 16.0 %collective-permute-start.2 = (bf16[64,5120]{1,0:T(8,128)(2,1)}, bf16[64,5120]{1,0:T(8,128)(2,1)}, u32[]{:S(2)}, u32[]{:S(2)}) collective-permute-start(bf16[64,5120]{1,0:T(8,128)(2,1)} %collective-permute-done.1), channel_id=1, source_target_pairs={{0,4},{1,5},{2,6},{3,7},{4,8},{5,9},{6,10},{7,11},{8,12},{9,13},{1... | collective-permute-start | bytes 1966088 | tf_op jit(solution)/shard_map/ppermute | solution.py:16
  318.7 8.2 %copy-start.5 = (bf16[256,512]{0,1:T(8,128)(2,1)S(1)}, bf16[256,512]{0,1:T(8,128)(2,1)}, u32[]{:S(2)}) copy-start(bf16[256,512]{0,1:T(8,128)(2,1)} %copy.119) | copy-start | bytes 786436
  335.5 1.3 copy-start.2
  342.9 1.3 copy-start.1
  349.7 1.3 copy-start
  356.4 1.2 copy-start.6
  356.4 1.9 copy-start.7
  376.7 1.8 copy-start.4
Sparse Core Ops, SparseCore 0:
  10.3 129.9 all-gather.1
where the time goes:
time: 391 us; the launch traced here: 389 us
  waiting for transfers between devices  243 us (62%)
  local copies, waits for them, and re-layouts  75.8 us (19%)
  matrix products  25.4 us (6%)
  starting transfers between devices  23.8 us (6%)
  between operations  15 us (4%)
  other arithmetic  5.91 us (2%)
    ppermute x6, waiting for transfers between devices, passed_along(): return lax.ppermute(value, axis, pairs)  243 us
    ppermute x6, starting transfers between devices, passed_along(): return lax.ppermute(value, axis, pairs)  23.7 us
    concatenate x1, local copies, waits for them, and re-layouts, shards(): key_rows = jnp.concatenate([sink_rows] + frame_parts, axis=0)  20.5 us
    unnamed x35, local copies, waits for them, and re-layouts  19.6 us
    dot_general x5, matrix products, blend_heads(): jnp.einsum('qhd,khd->hqk', query_block, key_block, preferred_element_type...  11.4 us
    slice x1, local copies, waits for them, and re-layouts, blend_heads(): key_block = key_rows[:, low:high].reshape(key_count, bundle, HDIM)  8.14 us
    dot_general x5, matrix products, blend_heads(): jnp.einsum('hqk,khd->qhd', weights.astype(jnp.bfloat16), value_block, pre...  7.99 us
  transfers between devices with their start and end apart: 7, of which 4 were waited for; matrix products, arithmetic and copies ran while one was open for 21% of the time, Pallas kernels for 0%

commit v1 on v0

v1 whole, which is shorter than its diff:
```python
import math

import jax
import jax.numpy as jnp
from jax import lax
from jax.experimental import pallas as pl
from jax.experimental.pallas import tpu as pltpu
from jax.sharding import PartitionSpec as P

HEADS = 20
HDIM = 128
WIN = 4
CHUNKS = 4
PER = HEADS // CHUNKS
CW = PER * HDIM
WIDTH = HEADS * HDIM
STAT = 16
LOG_SCALE = math.log2(math.e) / math.sqrt(HDIM)
VMEM = 48 * 1024 * 1024


def diagonal():
    rows = lax.broadcasted_iota(jnp.int32, (HDIM, HDIM), 0)
    cols = lax.broadcasted_iota(jnp.int32, (HDIM, HDIM), 1)
    return rows == cols


def stat_rows(column):
    eye = diagonal()
    groups = column.shape[0] // HDIM
    tops, mids, lows = [], [], []
    for group in range(groups):
        part = column[group * HDIM : (group + 1) * HDIM]
        row = jnp.sum(jnp.where(eye, part, 0.0), axis=0, keepdims=True)
        top = row.astype(jnp.bfloat16).astype(jnp.float32)
        mid = (row - top).astype(jnp.bfloat16).astype(jnp.float32)
        tops.append(top)
        mids.append(mid)
        lows.append(row - top - mid)
    used = tops + mids + lows
    used.append(jnp.zeros((STAT - len(used), HDIM), jnp.float32))
    return jnp.concatenate(used, axis=0).astype(jnp.bfloat16)


def stat_column(tile, groups):
    eye = diagonal()
    tile = tile.astype(jnp.float32)
    columns = []
    for group in range(groups):
        row = (
            tile[group : group + 1]
            + tile[groups + group : groups + group + 1]
            + tile[2 * groups + group : 2 * groups + group + 1]
        )
        columns.append(jnp.sum(jnp.where(eye, row, 0.0), axis=1, keepdims=True))
    return jnp.concatenate(columns, axis=0)


def fresh_state(query, keys, values):
    scores = lax.dot_general(
        query, keys, (((1,), (1,)), ((), ())), preferred_element_type=jnp.float32
    )
    top = jnp.max(scores, axis=1, keepdims=True)
    weights = jnp.exp2((scores - top) * LOG_SCALE)
    total = jnp.sum(weights, axis=1, keepdims=True)
    blended = jnp.dot(weights.astype(jnp.bfloat16), values, preferred_element_type=jnp.float32)
    return top * LOG_SCALE, total, blended


def merge_states(states):
    if len(states) == 1:
        return states[0]
    top = states[0][0]
    for state in states[1:]:
        top = jnp.maximum(top, state[0])
    total, blended = 0.0, 0.0
    for state in states:
        factor = jnp.exp2(state[0] - top)
        total = total + state[1] * factor
        blended = blended + state[2] * factor
    return top, total, blended


def stacked(refs):
    pieces = [ref[...] for ref in refs]
    return pieces[0] if len(pieces) == 1 else jnp.concatenate(pieces, axis=0)


class Block:
    def __init__(self, array, rows, index, base):
        self.array, self.rows, self.index, self.base = array, rows, index, base

    def spec(self):
        index, base = self.index, self.base
        return pl.BlockSpec((self.rows, HDIM), lambda head: (index, base + head))


def attend(queries, pairs, parts, heads, out_rows=None, final=None, name="attend"):
    count = len(queries)
    frame = queries[0].rows
    blocks = list(queries)
    for key, value in pairs:
        blocks += [key, value]
    blocks += parts
    operands = [block.array for block in blocks]
    in_specs = [block.spec() for block in blocks]
    aliases = {}
    if final is None:
        out_shape = jax.ShapeDtypeStruct((out_rows, heads * HDIM), jnp.bfloat16)
        out_specs = pl.BlockSpec((count * (frame + STAT), HDIM), lambda head: (0, head))
    else:
        onto, shape, base = final
        out_shape = jax.ShapeDtypeStruct(shape, jnp.bfloat16)
        out_specs = pl.BlockSpec((frame, HDIM), lambda head: (0, base + head))
        if onto is not None:
            aliases = {len(operands): 0}
            operands.append(onto)
            in_specs.append(pl.BlockSpec(memory_space=pl.ANY))

    def kernel(*refs):
        out = refs[-1]
        query_refs = refs[:count]
        key_refs = refs[count : count + 2 * len(pairs) : 2]
        value_refs = refs[count + 1 : count + 2 * len(pairs) : 2]
        part_refs = refs[count + 2 * len(pairs) : count + 2 * len(pairs) + len(parts)]
        if pairs:
            keys, values = stacked(key_refs), stacked(value_refs)
        for at in range(count):
            states = []
            if pairs:
                states.append(fresh_state(query_refs[at][...], keys, values))
            for part in part_refs:
                states.append(
                    (
                        stat_column(part[frame : frame + STAT], frame // HDIM),
                        1.0,
                        part[:frame].astype(jnp.float32),
                    )
                )
            top, total, blended = merge_states(states)
            rows = (blended / total).astype(jnp.bfloat16)
            if final is None:
                start = at * (frame + STAT)
                out[start : start + frame] = rows
                out[start + frame : start + frame + STAT] = stat_rows(top + jnp.log2(total))
            else:
                out[...] = rows

    key_rows = sum(key.rows for key, _ in pairs)
    return pl.pallas_call(
        kernel,
        out_shape=out_shape,
        grid=(heads,),
        in_specs=in_specs,
        out_specs=out_specs,
        input_output_aliases=aliases,
        compiler_params=pltpu.CompilerParams(vmem_limit_bytes=VMEM),
        cost_estimate=pl.CostEstimate(
            flops=4 * heads * count * frame * key_rows * HDIM,
            bytes_accessed=2 * heads * HDIM * (count * frame * 2 + 2 * key_rows),
            transcendentals=heads * count * frame * key_rows,
        ),
        name=name,
    )(*operands)


def chunk_rows(array):
    return jnp.concatenate(
        [array[:, at : at + CW] for at in range(0, array.shape[1], CW)], axis=0
    )


def fill(array, rows):
    if array.shape[0] == rows:
        return array
    return jnp.pad(array, ((0, rows - array.shape[0]), (0, 0)))


def shards(queries, cross_queries, frame_kv, sink_kv, prompt_kv, switch):
    streams = lax.axis_size("span") // WIN
    device = lax.axis_index("span")
    place = device // streams
    stream = device % streams
    frame = queries.shape[0]
    sink = sink_kv.reshape(sink_kv.shape[1], sink_kv.shape[2])
    sink_rows = sink.shape[0]
    prompt_rows = prompt_kv.shape[1]
    part_rows = frame + STAT
    kvs_rows = 2 * frame + 2 * sink_rows
    prompt = chunk_rows(prompt_kv.reshape(-1, prompt_kv.shape[2]))
    own_sink = chunk_rows(sink)

    def move(value, pairs):
        both = [(a * streams + s, b * streams + s) for a, b in pairs for s in range(streams)]
        return lax.ppermute(value, "span", both)

    def across(value, flip):
        pairs = [(at, (at // streams) * streams + ((at % streams) ^ flip)) for at in range(WIN * streams)]
        return lax.ppermute(value, "span", pairs)

    def choose(branches, *operands):
        return lax.switch(place, branches, *operands)

    def query_cols(array, *chunks):
        return jnp.concatenate([array[:, c * CW : (c + 1) * CW] for c in chunks], axis=0)

    def kvs(chunk):
        low = chunk * CW
        return jnp.concatenate(
            [
                frame_kv[:, low : low + CW],
                frame_kv[:, WIDTH + low : WIDTH + low + CW],
                sink[:, low : low + CW],
                sink[:, WIDTH + low : WIDTH + low + CW],
            ],
            axis=0,
        )

    def own_query(array, chunk):
        return Block(array, frame, 0, chunk * PER)

    def own_pairs(frame_array, sink_array, chunk):
        base = chunk * PER
        return [
            (Block(frame_array, frame, 0, base), Block(frame_array, frame, 0, HEADS + base)),
            (Block(sink_array, sink_rows, 0, base), Block(sink_array, sink_rows, 0, HEADS + base)),
        ]

    def kvs_pairs(array):
        first = 2 * frame // sink_rows
        return [
            (Block(array, frame, 0, 0), Block(array, frame, 1, 0)),
            (Block(array, sink_rows, first, 0), Block(array, sink_rows, first + 1, 0)),
        ]

    def sink_pair(array, chunk):
        return (
            Block(array, sink_rows, chunk, 0),
            Block(array, sink_rows, CHUNKS + chunk, 0),
        )

    def part(array, index):
        return Block(array, part_rows, index, 0)

    stream_ids = jnp.arange(switch.shape[0], dtype=jnp.int32)

    def picked_by(which):
        at = jnp.sum(jnp.where(stream_ids == which, switch, 0))
        return (place >= at).astype(jnp.int32)

    pick, other_pick = picked_by(stream), picked_by(stream ^ 1)

    def spread(shard):
        held = [shard]
        flip = streams // 2
        while flip > 1:
            held = held + [across(each, flip) for each in held]
            flip //= 2

        def chosen(which):
            parts = [
                lax.dynamic_index_in_dim(
                    each.reshape(2 * CHUNKS, 2, prompt_rows, CW), which, 1, keepdims=False
                )
                for each in held
            ]
            return jnp.concatenate(parts, axis=1).reshape(-1, CW)

        return chosen(pick), across(chosen(other_pick), 1)

    prompt_size = prompt.shape[0]
    same = max(prompt_size, 2 * frame, own_sink.shape[0])
    wide = max(kvs_rows, prompt_size, 2 * part_rows)

    up1 = move(prompt, [(0, 1), (1, 2), (2, 3)])
    down1 = move(
        choose(
            [
                lambda q, p: fill(p, same),
                lambda q, p: fill(p, same),
                lambda q, p: fill(query_cols(q, 0, 1), same),
                lambda q, p: fill(p, same),
            ],
            queries,
            prompt,
        ),
        [(3, 2), (2, 1), (1, 0)],
    )
    up2 = move(
        jnp.where(place == 0, kvs(0), kvs(3)),
        [(0, 1), (1, 2)],
    )
    down2 = move(
        choose(
            [
                lambda q, s: fill(s, same),
                lambda q, s: fill(s, same),
                lambda q, s: fill(s, same),
                lambda q, s: fill(query_cols(q, 0, 1), same),
            ],
            queries,
            own_sink,
        ),
        [(3, 1), (1, 0)],
    )
    stages = [spread(prompt)]
    home = attend(
        [own_query(queries, 0)],
        own_pairs(frame_kv, sink, 0),
        [],
        HEADS,
        out_rows=part_rows,
        name="home",
    )
    up3 = move(
        choose(
            [lambda k, r: fill(k, wide)] + [lambda k, r: fill(r, wide)] * 3,
            kvs(3),
            up1,
        ),
        [(0, 1), (1, 2), (2, 3)],
    )
    down3 = move(
        choose(
            [lambda q, p: fill(p, same)] * 3 + [lambda q, p: fill(query_cols(q, 2, 3), same)],
            queries,
            prompt,
        ),
        [(3, 2), (2, 1)],
    )
    stages.append(
        spread(jnp.where(place == 0, down1[:prompt_size], up1))
    )

    def visit(q2, q3, came, frame_array, sink_array, chunk):
        return attend(
            [q2, q3],
            own_pairs(frame_array, sink_array, chunk) + kvs_pairs(came),
            [],
            PER,
            out_rows=wide,
            name="visit",
        )

    up4 = move(
        choose(
            [lambda k, f, s, c, d1, d2: fill(k, wide)]
            + [
                lambda k, f, s, c, d1, d2: visit(
                    Block(d1, frame, 0, 0), Block(d2, frame, 0, 0), c, f, s, 0
                )
            ]
            + [lambda k, f, s, c, d1, d2: fill(k, wide)] * 2,
            kvs(1),
            frame_kv,
            sink,
            up2,
            down1,
            down2,
        ),
        [(0, 1), (1, 2)],
    )
    down4 = move(
        choose(
            [lambda q, r: r] * 3 + [lambda q, r: fill(query_cols(q, 0, 1), same)],
            queries,
            down1,
        ),
        [(3, 2), (2, 1)],
    )
    up5 = move(
        choose(
            [lambda k, r: fill(k, wide)] + [lambda k, r: r] * 3,
            kvs(2),
            up3,
        ),
        [(0, 1), (1, 2), (2, 3)],
    )
    down5 = move(
        choose(
            [
                lambda q, s, r: r,
                lambda q, s, r: r,
                lambda q, s, r: fill(
                    jnp.concatenate([q[:, 2 * CW : 3 * CW], r[:frame]], axis=0), same
                ),
                lambda q, s, r: fill(s, same),
            ],
            queries,
            own_sink,
            down3,
        ),
        [(3, 2), (2, 1), (1, 0)],
    )
    stages.append(
        spread(
            choose(
                [
                    lambda u3, d1, d3, d5: d5[:prompt_size],
                    lambda u3, d1, d3, d5: d3[:prompt_size],
                    lambda u3, d1, d3, d5: d1[:prompt_size],
                    lambda u3, d1, d3, d5: u3[:prompt_size],
                ],
                up3,
                down1,
                down3,
                down5,
            )
        )
    )

    def join(query, came, frame_array, sink_array, chunk, rows):
        return attend(
            [query],
            own_pairs(frame_array, sink_array, chunk),
            [part(came, 1)],
            PER,
            out_rows=rows,
            name="join",
        )

    two = 2 * part_rows
    up6 = move(
        choose(
            [lambda f, s, u4, d1, d2, d4: jnp.zeros((two, CW), jnp.bfloat16)]
            + [
                lambda f, s, u4, d1, d2, d4: attend(
                    [Block(d1, frame, 1, 0), Block(d2, frame, 1, 0)],
                    own_pairs(f, s, 1) + kvs_pairs(u4),
                    [],
                    PER,
                    out_rows=two,
                    name="visit",
                )
            ]
            + [lambda f, s, u4, d1, d2, d4: join(Block(d4, frame, 0, 0), u4, f, s, 0, two)]
            + [lambda f, s, u4, d1, d2, d4: jnp.zeros((two, CW), jnp.bfloat16)],
            frame_kv,
            sink,
            up4,
            down1,
            down2,
            down4,
        ),
        [(1, 2), (2, 3)],
    )
    down6 = move(
        choose(
            [lambda s, r: r] * 2 + [lambda s, r: fill(s, same)] * 2,
            own_sink,
            down4,
        ),
        [(2, 1), (1, 0)],
    )
    stages.append(
        spread(
            choose(
                [
                    lambda u3, u5, d4, d6: d6[:prompt_size],
                    lambda u3, u5, d4, d6: d4[:prompt_size],
                    lambda u3, u5, d4, d6: u3[:prompt_size],
                    lambda u3, u5, d4, d6: u5[:prompt_size],
                ],
                up3,
                up5,
                down4,
                down6,
            )
        )
    )
    up7 = move(
        choose(
            [lambda f, s, u2, u5, d3, d5: jnp.zeros((two, CW), jnp.bfloat16)]
            + [
                lambda f, s, u2, u5, d3, d5: attend(
                    [Block(d5, frame, 0, 0), Block(d5, frame, 1, 0)],
                    own_pairs(f, s, 2) + kvs_pairs(u5),
                    [],
                    PER,
                    out_rows=two,
                    name="visit",
                )
            ]
            + [
                lambda f, s, u2, u5, d3, d5: attend(
                    [Block(d3, frame, 1, 0)],
                    own_pairs(f, s, 3) + kvs_pairs(u2) + kvs_pairs(u5),
                    [],
                    PER,
                    out_rows=two,
                    name="all_d",
                )
            ]
            + [lambda f, s, u2, u5, d3, d5: jnp.zeros((two, CW), jnp.bfloat16)],
            frame_kv,
            sink,
            up2,
            up5,
            down3,
            down5,
        ),
        [(1, 2), (2, 3)],
    )
    down7 = move(down5, [(2, 1)])
    last8 = move(
        choose(
            [lambda f, s, u6, d4, d6: d6] * 2
            + [lambda f, s, u6, d4, d6: join(Block(d4, frame, 1, 0), u6, f, s, 1, same)]
            + [lambda f, s, u6, d4, d6: d6],
            frame_kv,
            sink,
            up6,
            down4,
            down6,
        ),
        [(2, 3), (1, 0)],
    )
    down9 = move(down7, [(1, 0)])
    up9 = move(
        choose(
            [lambda f, s, u7, d3: jnp.zeros((part_rows, CW), jnp.bfloat16)] * 2
            + [lambda f, s, u7, d3: join(Block(d3, frame, 0, 0), u7, f, s, 2, part_rows)]
            + [lambda f, s, u7, d3: jnp.zeros((part_rows, CW), jnp.bfloat16)],
            frame_kv,
            sink,
            up7,
            down3,
        ),
        [(2, 3)],
    )

    mine = [stage[0] for stage in stages]
    theirs = [stage[1] for stage in stages]
    cross_out = cross(cross_queries, mine + theirs)

    def finish(q, h, pairs_of, parts_of):
        out = None
        for chunk in range(CHUNKS):
            out = attend(
                [own_query(q, chunk)],
                pairs_of(chunk),
                [Block(h, part_rows, 0, chunk * PER)] + parts_of(chunk),
                PER,
                final=(out, q.shape, chunk * PER),
                name="finish",
            )
        return out

    def finish0(q, h, u, d, l8, d9, u9):
        late = [d[2], l8, d9]
        return finish(q, h, lambda c: [sink_pair(each, c) for each in late], lambda c: [])

    def finish1(q, h, u, d, l8, d9, u9):
        late = [d[6], d[7]]
        came = [u[2], u[4], u[5], u[3]]
        return finish(
            q,
            h,
            lambda c: kvs_pairs(came[c]) + [sink_pair(each, c) for each in late],
            lambda c: [],
        )

    def finish2(q, h, u, d, l8, d9, u9):
        came = [u[4], u[6], u[7]]
        return finish(
            q,
            h,
            lambda c: [sink_pair(d[5], c)] + ((kvs_pairs(u[2]) + kvs_pairs(u[5])) if c == 3 else []),
            lambda c: [part(came[c], 0)] if c < 3 else [],
        )

    def finish3(q, h, u, d, l8, d9, u9):
        came = [u[6], l8, u9, u[7]]
        return finish(q, h, lambda c: [], lambda c: [part(came[c], 0)])

    ups = {2: up2, 3: up3, 4: up4, 5: up5, 6: up6, 7: up7}
    downs = {2: down2, 5: down5, 6: down6, 7: down7}
    self_out = choose(
        [finish0, finish1, finish2, finish3], queries, home, ups, downs, last8, down9, up9
    )
    return (self_out, cross_out)


def cross(queries, arrays):
    frame = queries.shape[0]

    def kernel(*refs):
        query, out = refs[0], refs[-1]
        keys, values = stacked(refs[1:-1:2]), stacked(refs[2:-1:2])
        _, total, blended = fresh_state(query[...], keys, values)
        out[...] = (blended / total).astype(jnp.bfloat16)

    operands, in_specs = [queries], [pl.BlockSpec((frame, HDIM), lambda head: (0, head))]
    for array in arrays:
        rows = array.shape[0] // (2 * CHUNKS)
        operands += [array, array]
        in_specs += [
            pl.BlockSpec((rows, HDIM), lambda head: (head // PER, head % PER)),
            pl.BlockSpec((rows, HDIM), lambda head: (CHUNKS + head // PER, head % PER)),
        ]
    key_rows = sum(array.shape[0] for array in arrays) // (2 * CHUNKS)
    return pl.pallas_call(
        kernel,
        out_shape=jax.ShapeDtypeStruct(queries.shape, jnp.bfloat16),
        grid=(HEADS,),
        in_specs=in_specs,
        out_specs=pl.BlockSpec((frame, HDIM), lambda head: (0, head)),
        compiler_params=pltpu.CompilerParams(vmem_limit_bytes=VMEM),
        cost_estimate=pl.CostEstimate(
            flops=4 * HEADS * frame * key_rows * HDIM,
            bytes_accessed=2 * WIDTH * (2 * frame + 2 * key_rows),
            transcendentals=HEADS * frame * key_rows,
        ),
        name="cross",
    )(*operands)


def solution(mesh):
    in_specs = (
        P(("groups", "span"), None),
        P(("groups", "span"), None),
        P(("groups", "span"), None),
        P(("groups", "span"), None, None),
        P("groups", "span", None),
        P("groups"),
    )
    out_specs = (P(("groups", "span"), None), P(("groups", "span"), None))
    return jax.shard_map(shards, mesh=mesh, in_specs=in_specs, out_specs=out_specs, check_vma=False)
```

time: 391 us -> 223 us (0.57)
  the two profiles are of different devices: /device:TPU:0 before, /device:TPU:16 now
where the time goes in v1:
time: 223 us; the launch traced here: 220 us
  Pallas kernels  75.9 us (34%)
  local copies, waits for them, and re-layouts  49.6 us (22%)
  starting transfers between devices  45.1 us (20%)
  waiting for transfers between devices  32.5 us (15%)
  other arithmetic  14.2 us (6%)
  between operations  2.3 us (1%)
    pallas_call x9, Pallas kernels, attend(): pl.pallas_call(kernel, out_shape=out_shape, grid=(heads,), in_specs=in_sp...  60.8 us
    ppermute x17, starting transfers between devices, move(): return lax.ppermute(value, 'span', both)  38.9 us
    ppermute x17, waiting for transfers between devices, move(): return lax.ppermute(value, 'span', both)  29.7 us
    unnamed x59, local copies, waits for them, and re-layouts  16.5 us
    pallas_call x1, Pallas kernels, cross(): pl.pallas_call(kernel, out_shape=jax.ShapeDtypeStruct(queries.shape, jnp....  15.1 us
    cond x8, local copies, waits for them, and re-layouts  11.2 us
    squeeze x6, local copies, waits for them, and re-layouts, chosen(): lax.dynamic_index_in_dim(each.reshape(2 * CHUNKS, 2, prompt_rows, CW), wh...  10.5 us
    ppermute x8, starting transfers between devices, across(): return lax.ppermute(value, 'span', pairs)  6.19 us
  transfers between devices with their start and end apart: 25, of which 5 were waited for; matrix products, arithmetic and copies ran while one was open for 23% of the time, Pallas kernels for 28%

profile of v1, /device:TPU:16, one launch (start us, length us, event | category | flops | bytes accessed | tf_op | source)
XLA Modules:
  0.0 219.8 jit_solution(260049301353917423)
XLA Ops:
  13.0 3.5 %collective-permute-start.12 = (bf16[512,640]{1,0:T(8,128)(2,1)}, bf16[512,640]{1,0:T(8,128)(2,1)}, u32[]{:S(2)}, u32[]{:S(2)}) collective-permute-start(bf16[512,640]{1,0:T(8,128)(2,1)} %slice_dynamic-update-slice_fusion), channel_id=1, source_target_pairs={{0,4},{1,5},{2,6},{3,7},{4,8},{5,9},{6,10},{7,11},{8,12},{9,13},{1... | collective-permute-start | bytes 1966088 | tf_op jit(solution)/shard_map/ppermute | solution.py:195
  35.7 5.0 %collective-permute-start.13 = (bf16[640,640]{1,0:T(8,128)(2,1)}, bf16[640,640]{1,0:T(8,128)(2,1)}, u32[]{:S(2)}, u32[]{:S(2)}) collective-permute-start(bf16[640,640]{1,0:T(8,128)(2,1)} %get-tuple-element.383), channel_id=1, source_target_pairs={{0,4},{1,5},{2,6},{3,7},{4,8},{5,9},{6,10},{7,11},{8,12},{9,13},{1... | collective-permute-start | bytes 2457608 | tf_op jit(solution)/shard_map/ppermute | solution.py:195
  44.8 7.7 %collective-permute-done.1 = bf16[512,640]{1,0:T(8,128)(2,1)} collective-permute-done((bf16[512,640]{1,0:T(8,128)(2,1)}, bf16[512,640]{1,0:T(8,128)(2,1)}, u32[]{:S(2)}, u32[]{:S(2)}) %collective-permute-start.1) | collective-permute-done | bytes 655392 | tf_op jit(solution)/shard_map/ppermute | solution.py:195
  56.5 2.9 %conditional.24 = (bf16[512,640]{1,0:T(8,128)(2,1)}) conditional(s32[]{:T(128)} %clamp.2, bf16[512,640]{1,0:T(8,128)(2,1)} %collective-permute-done.8, bf16[512,640]{1,0:T(8,128)(2,1)} %collective-permute-done.8, (bf16[256,2560]{1,0:T(8,128)(2,1)}, bf16[512,640]{1,0:T(8,128)(2,1)}) %tuple.242, ...), branch_computations={%region_32.33_spmd, %region_33.34_spmd, %region_34.35_spmd, %regio... | conditional | flops 1310720 | bytes 2621448 | solution.py:202
  67.5 13.3 %collective-permute-done.2 = bf16[512,640]{1,0:T(8,128)(2,1)} collective-permute-done((bf16[512,640]{1,0:T(8,128)(2,1)}, bf16[512,640]{1,0:T(8,128)(2,1)}, u32[]{:S(2)}, u32[]{:S(2)}) %collective-permute-start.2) | collective-permute-done | bytes 655392 | tf_op jit(solution)/shard_map/ppermute | solution.py:195
  82.7 2.8 %collective-permute-start.3 = (bf16[512,640]{1,0:T(8,128)(2,1)}, bf16[512,640]{1,0:T(8,128)(2,1)}, u32[]{:S(2)}, u32[]{:S(2)}) collective-permute-start(bf16[512,640]{1,0:T(8,128)(2,1)} %get-tuple-element.377), channel_id=1, source_target_pairs={{8,4},{9,5},{10,6},{11,7},{4,0},{5,1},{6,2},{7,3},{24,20},{25,21},... | collective-permute-start | bytes 1966088 | tf_op jit(solution)/shard_map/ppermute | solution.py:195
  96.8 4.2 %collective-permute-start.10 = (bf16[512,640]{1,0:T(8,128)(2,1)}, bf16[512,640]{1,0:T(8,128)(2,1)}, u32[]{:S(2)}, u32[]{:S(2)}) collective-permute-start(bf16[512,640]{1,0:T(8,128)(2,1)} %collective-permute-done.9), channel_id=1, source_target_pairs={{8,4},{9,5},{10,6},{11,7},{24,20},{25,21},{26,22},{27,23}} | collective-permute-start | bytes 1966088 | tf_op jit(solution)/shard_map/ppermute | solution.py:195
  103.1 6.5 %conditional.21 = (bf16[544,640]{1,0:T(8,128)(2,1)}) conditional(s32[]{:T(128)} %clamp.2, () %tuple.236, (bf16[512,640]{1,0:T(8,128)(2,1)}, bf16[512,640]{1,0:T(8,128)(2,1)}, bf16[256,5120]{1,0:T(8,128)(2,1)S(1)}, bf16[64,5120]{1,0:T(8,128)(2,1)}, bf16[640,640]{1,0:T(8,128)(2,1)}) %tuple.369, ...), branch_computations={%region_20.21_spmd, %region_21.22_spmd, %region_22.23_spmd, %regio... | conditional | flops 838860800 | bytes 2949128 | solution.py:202
  103.1 6.5 %join.3 = bf16[544,640]{1,0:T(8,128)(2,1)} custom-call(bf16[512,640]{1,0:T(8,128)(2,1)} %get-tuple-element.273.refs_0_, bf16[256,5120]{1,0:T(8,128)(2,1)S(1)} %get-tuple-element.274.refs_1_.refs_2_, bf16[256,5120]{1,0:T(8,128)(2,1)S(1)} %get-tuple-element.274.refs_1_.refs_2_, bf16[64,5120]{1,0:T(8,128)(2,1)} %get-tuple-element.275.refs_3_.refs_4_, ...), custom_call_target="tpu_custom_call" | custom-call | flops 209715200 | bytes 1474560 | tf_op jit(solution)/shard_map/cond/branch_2_fun/join/pallas_call | solution.py:150
  122.8 5.6 %conditional.27 = (bf16[544,640]{1,0:T(8,128)(2,1)}) conditional(s32[]{:T(128)} %clamp.2, () %tuple.245, (bf16[512,640]{1,0:T(8,128)(2,1)}, bf16[256,5120]{1,0:T(8,128)(2,1)S(1)}, bf16[64,5120]{1,0:T(8,128)(2,1)}, bf16[640,640]{1,0:T(8,128)(2,1)S(1)}) %tuple.371, (bf16[512,640]{1,0:T(8,128)(2,1)}, ...), branch_computations={%region_44.45_spmd, %region_45.46_spmd, %region_46.47_spmd, %regio... | conditional | flops 838860800 | bytes 3112968 | solution.py:202
  122.8 5.6 %all_d.1 = bf16[544,640]{1,0:T(8,128)(2,1)} custom-call(bf16[512,640]{1,0:T(8,128)(2,1)} %get-tuple-element.287.refs_0_, bf16[256,5120]{1,0:T(8,128)(2,1)S(1)} %get-tuple-element.288.refs_1_.refs_2_, bf16[256,5120]{1,0:T(8,128)(2,1)S(1)} %get-tuple-element.288.refs_1_.refs_2_, bf16[64,5120]{1,0:T(8,128)(2,1)} %get-tuple-element.289.refs_3_.refs_4_, ...), custom_call_target="tpu_custom_call" | custom-call | flops 629145600 | bytes 3112960 | tf_op jit(solution)/shard_map/cond/branch_2_fun/all_d/pallas_call | solution.py:150
  136.0 6.6 %conditional.22 = (bf16[512,640]{1,0:T(8,128)(2,1)}) conditional(s32[]{:T(128)} %clamp.2, bf16[512,640]{1,0:T(8,128)(2,1)} %collective-permute-done.3, bf16[512,640]{1,0:T(8,128)(2,1)} %collective-permute-done.3, (bf16[512,640]{1,0:T(8,128)(2,1)}, bf16[256,5120]{1,0:T(8,128)(2,1)S(1)}, bf16[64,5120]{1,0:T(8,128)(2,1)}, ...), branch_computations={%region_24.25_spmd, %region_25.26_spmd, %region_26.27_spmd, %regio... | conditional | flops 209715200 | bytes 1474568 | solution.py:202
  136.0 6.6 %join.4 = bf16[512,640]{1,0:T(8,128)(2,1)} custom-call(bf16[512,640]{1,0:T(8,128)(2,1)} %get-tuple-element.277.refs_0_, bf16[256,5120]{1,0:T(8,128)(2,1)S(1)} %get-tuple-element.278.refs_1_.refs_2_, bf16[256,5120]{1,0:T(8,128)(2,1)S(1)} %get-tuple-element.278.refs_1_.refs_2_, bf16[64,5120]{1,0:T(8,128)(2,1)} %get-tuple-element.279.refs_3_.refs_4_, ...), custom_call_target="tpu_custom_call" | custom-call | flops 209715200 | bytes 1474560 | tf_op jit(solution)/shard_map/cond/branch_2_fun/join/pallas_call | solution.py:150
  143.1 2.8 %collective-permute-done.20 = bf16[512,640]{1,0:T(8,128)(2,1)} collective-permute-done((bf16[512,640]{1,0:T(8,128)(2,1)}, bf16[512,640]{1,0:T(8,128)(2,1)}, u32[]{:S(2)}, u32[]{:S(2)}) %collective-permute-start.20) | collective-permute-done | bytes 655392 | tf_op jit(solution)/shard_map/ppermute | solution.py:199
  152.8 12.2 %home.1 = bf16[272,2560]{1,0:T(8,128)(2,1)} custom-call(bf16[256,2560]{1,0:T(8,128)(2,1)S(1)} %copy-done.2, bf16[256,5120]{1,0:T(8,128)(2,1)S(1)} %copy-done, bf16[256,5120]{1,0:T(8,128)(2,1)S(1)} %copy-done, bf16[64,5120]{1,0:T(8,128)(2,1)S(1)} %bitcast.72, bf16[64,5120]{1,0:T(8,128)(2,1)S(1)} %bitcast.73), custom_call_target="tpu_custom_call" | custom-call | flops 838860800 | bytes 5898240 | tf_op jit(solution)/shard_map/home/pallas_call | solution.py:150
  165.1 6.6 %conditional.28 = (bf16[272,640]{1,0:T(8,128)(2,1)}) conditional(s32[]{:T(128)} %clamp.2, () %tuple.250, () %tuple.251, (bf16[512,640]{1,0:T(8,128)(2,1)}, bf16[256,5120]{1,0:T(8,128)(2,1)}, bf16[64,5120]{1,0:T(8,128)(2,1)S(1)}, bf16[544,640]{1,0:T(8,128)(2,1)}) %tuple.375, () %tuple.253), branch_computations={%region_48.49_spmd, %region_49.50_spmd, %region_50.51_spmd, %regio... | conditional | flops 209715200 | bytes 1474568 | solution.py:202
  165.1 6.6 %join.5 = bf16[272,640]{1,0:T(8,128)(2,1)} custom-call(bf16[512,640]{1,0:T(8,128)(2,1)} %get-tuple-element.292.refs_0_, bf16[256,5120]{1,0:T(8,128)(2,1)} %get-tuple-element.293.refs_1_.refs_2_, bf16[256,5120]{1,0:T(8,128)(2,1)} %get-tuple-element.293.refs_1_.refs_2_, bf16[64,5120]{1,0:T(8,128)(2,1)S(1)} %get-tuple-element.294.refs_3_.refs_4_, ...), custom_call_target="tpu_custom_call" | custom-call | flops 209715200 | bytes 1474560 | tf_op jit(solution)/shard_map/cond/branch_2_fun/join/pallas_call | solution.py:150
  174.3 7.0 %collective-permute-done.16 = bf16[272,640]{1,0:T(8,128)(2,1)S(1)} collective-permute-done((bf16[272,640]{1,0:T(8,128)(2,1)}, bf16[272,640]{1,0:T(8,128)(2,1)S(1)}, u32[]{:S(2)}, u32[]{:S(2)}) %collective-permute-start.16) | collective-permute-done | bytes 348192 | tf_op jit(solution)/shard_map/ppermute | solution.py:195
  181.3 23.3 %conditional.29 = (bf16[256,2560]{1,0:T(8,128)(2,1)}) conditional(s32[]{:T(128)} %clamp.2, (bf16[256,2560]{1,0:T(8,128)(2,1)S(1)}, bf16[512,640]{1,0:T(8,128)(2,1)}, bf16[512,640]{1,0:T(8,128)(2,1)}, bf16[512,640]{1,0:T(8,128)(2,1)}, bf16[272,2560]{1,0:T(8,128)(2,1)S(1)}) %tuple.363, ...), branch_computations={%region_52.53_spmd, %region_53.54_spmd, %region_54.55_spmd, %regio... | conditional | flops 1174405120 | bytes 10485796 | solution.py:202
  181.3 5.5 %finish.24.refs_5_ = bf16[256,2560]{1,0:T(8,128)(2,1)} custom-call(bf16[256,2560]{1,0:T(8,128)(2,1)S(1)} %get-tuple-element.309.refs_0_, bf16[512,640]{1,0:T(8,128)(2,1)} %get-tuple-element.310.refs_1_.refs_2_, bf16[512,640]{1,0:T(8,128)(2,1)} %get-tuple-element.310.refs_1_.refs_2_, bf16[272,2560]{1,0:T(8,128)(2,1)S(1)} %get-tuple-element.313.refs_3_.refs_11_, ...), custom_call_target="tpu_custom_call" | custom-call | flops 41943040 | bytes 819200 | tf_op jit(solution)/shard_map/cond/branch_2_fun/finish/pallas_call | solution.py:150
  186.8 5.5 %finish.25.refs_5_ = bf16[256,2560]{1,0:T(8,128)(2,1)} custom-call(bf16[256,2560]{1,0:T(8,128)(2,1)S(1)} %get-tuple-element.309.refs_0_, bf16[512,640]{1,0:T(8,128)(2,1)} %get-tuple-element.310.refs_1_.refs_2_, bf16[512,640]{1,0:T(8,128)(2,1)} %get-tuple-element.310.refs_1_.refs_2_, ...), custom_call_target="tpu_custom_call", output_to_operand_aliasing={{}: (5, {})} | custom-call | flops 41943040 | bytes 819200 | tf_op jit(solution)/shard_map/cond/branch_2_fun/finish/pallas_call | solution.py:150
  192.3 5.6 %finish.26.refs_12_ = bf16[256,2560]{1,0:T(8,128)(2,1)} custom-call(bf16[256,2560]{1,0:T(8,128)(2,1)S(1)} %get-tuple-element.309.refs_0_, bf16[512,640]{1,0:T(8,128)(2,1)} %get-tuple-element.310.refs_1_.refs_2_, bf16[512,640]{1,0:T(8,128)(2,1)} %get-tuple-element.310.refs_1_.refs_2_, ...), custom_call_target="tpu_custom_call", output_to_operand_aliasing={{}: (5, {})} | custom-call | flops 41943040 | bytes 819200 | tf_op jit(solution)/shard_map/cond/branch_2_fun/finish/pallas_call | solution.py:150
  197.9 6.8 %finish.27 = bf16[256,2560]{1,0:T(8,128)(2,1)} custom-call(bf16[256,2560]{1,0:T(8,128)(2,1)S(1)} %get-tuple-element.309.refs_0_, bf16[512,640]{1,0:T(8,128)(2,1)} %get-tuple-element.310.refs_1_.refs_2_, bf16[512,640]{1,0:T(8,128)(2,1)} %get-tuple-element.310.refs_1_.refs_2_, ...), custom_call_target="tpu_custom_call", output_to_operand_aliasing={{}: (12, {})} | custom-call | flops 461373440 | bytes 2457600 | tf_op jit(solution)/shard_map/cond/branch_2_fun/finish/pallas_call | solution.py:150
  204.7 15.1 %cross.1 = bf16[256,2560]{1,0:T(8,128)(2,1)} custom-call(bf16[256,2560]{1,0:T(8,128)(2,1)} %refs_0_.3, bf16[512,640]{1,0:T(8,128)(2,1)S(1)} %bitcast.52, bf16[512,640]{1,0:T(8,128)(2,1)S(1)} %bitcast.53, bf16[512,640]{1,0:T(8,128)(2,1)S(1)} %bitcast.50, bf16[512,640]{1,0:T(8,128)(2,1)S(1)} %bitcast.51, bf16[512,640]{1,0:T(8,128)(2,1)S(1)} %bitcast.56, ...), custom_call_target="tpu_custom_call" | custom-call | flops 1342177280 | bytes 7864320 | tf_op jit(solution)/shard_map/cross/pallas_call | solution.py:602
  (149 shorter events, 112.5 us)
Async XLA Ops:
  13.0 20.7 %collective-permute-start.12 = (bf16[512,640]{1,0:T(8,128)(2,1)}, bf16[512,640]{1,0:T(8,128)(2,1)}, u32[]{:S(2)}, u32[]{:S(2)}) collective-permute-start(bf16[512,640]{1,0:T(8,128)(2,1)} %slice_dynamic-update-slice_fusion), channel_id=1, source_target_pairs={{0,4},{1,5},{2,6},{3,7},{4,8},{5,9},{6,10},{7,11},{8,12},{9,13},{1... | collective-permute-start | bytes 1966088 | tf_op jit(solution)/shard_map/ppermute | solution.py:195
  18.5 37.9 %collective-permute-start.8 = (bf16[512,640]{1,0:T(8,128)(2,1)}, bf16[512,640]{1,0:T(8,128)(2,1)}, u32[]{:S(2)}, u32[]{:S(2)}) collective-permute-start(bf16[512,640]{1,0:T(8,128)(2,1)} %get-tuple-element.381), channel_id=1, source_target_pairs={{12,8},{13,9},{14,10},{15,11},{8,4},{9,5},{10,6},{11,7},{28,24},{2... | collective-permute-start | bytes 1966088 | tf_op jit(solution)/shard_map/ppermute | solution.py:195
  23.2 29.3 %collective-permute-start.1 = (bf16[512,640]{1,0:T(8,128)(2,1)}, bf16[512,640]{1,0:T(8,128)(2,1)}, u32[]{:S(2)}, u32[]{:S(2)}) collective-permute-start(bf16[512,640]{1,0:T(8,128)(2,1)} %get-tuple-element.375), channel_id=1, source_target_pairs={{12,8},{13,9},{14,10},{15,11},{8,4},{9,5},{10,6},{11,7},{4,0},{5,1... | collective-permute-start | bytes 1966088 | tf_op jit(solution)/shard_map/ppermute | solution.py:195
  28.5 34.8 %collective-permute-start.4 = (bf16[640,640]{1,0:T(8,128)(2,1)}, bf16[640,640]{1,0:T(8,128)(2,1)}, u32[]{:S(2)}, u32[]{:S(2)}) collective-permute-start(bf16[640,640]{1,0:T(8,128)(2,1)} %get-tuple-element.344), channel_id=1, source_target_pairs={{0,4},{1,5},{2,6},{3,7},{4,8},{5,9},{6,10},{7,11},{16,20},{17,21},... | collective-permute-start | bytes 2457608 | tf_op jit(solution)/shard_map/ppermute | solution.py:195
  35.7 49.9 %collective-permute-start.13 = (bf16[640,640]{1,0:T(8,128)(2,1)}, bf16[640,640]{1,0:T(8,128)(2,1)}, u32[]{:S(2)}, u32[]{:S(2)}) collective-permute-start(bf16[640,640]{1,0:T(8,128)(2,1)} %get-tuple-element.383), channel_id=1, source_target_pairs={{0,4},{1,5},{2,6},{3,7},{4,8},{5,9},{6,10},{7,11},{8,12},{9,13},{1... | collective-permute-start | bytes 2457608 | tf_op jit(solution)/shard_map/ppermute | solution.py:195
  43.4 20.0 %collective-permute-start = (bf16[512,640]{1,0:T(8,128)(2,1)}, bf16[512,640]{1,0:T(8,128)(2,1)}, u32[]{:S(2)}, u32[]{:S(2)}) collective-permute-start(bf16[512,640]{1,0:T(8,128)(2,1)} %get-tuple-element.374), channel_id=1, source_target_pairs={{12,4},{13,5},{14,6},{15,7},{4,0},{5,1},{6,2},{7,3},{28,20},{29,21... | collective-permute-start | bytes 1966088 | tf_op jit(solution)/shard_map/ppermute | solution.py:195
  54.5 26.2 %collective-permute-start.2 = (bf16[512,640]{1,0:T(8,128)(2,1)}, bf16[512,640]{1,0:T(8,128)(2,1)}, u32[]{:S(2)}, u32[]{:S(2)}) collective-permute-start(bf16[512,640]{1,0:T(8,128)(2,1)} %get-tuple-element.376), channel_id=1, source_target_pairs={{12,8},{13,9},{14,10},{15,11},{8,4},{9,5},{10,6},{11,7},{28,24},{2... | collective-permute-start | bytes 1966088 | tf_op jit(solution)/shard_map/ppermute | solution.py:195
  59.4 33.9 %collective-permute-start.9 = (bf16[512,640]{1,0:T(8,128)(2,1)}, bf16[512,640]{1,0:T(8,128)(2,1)}, u32[]{:S(2)}, u32[]{:S(2)}) collective-permute-start(bf16[512,640]{1,0:T(8,128)(2,1)} %get-tuple-element.382), channel_id=1, source_target_pairs={{12,8},{13,9},{14,10},{15,11},{8,4},{9,5},{10,6},{11,7},{4,0},{5,1... | collective-permute-start | bytes 1966088 | tf_op jit(solution)/shard_map/ppermute | solution.py:195
  63.4 33.4 %collective-permute-start.5 = (bf16[640,640]{1,0:T(8,128)(2,1)}, bf16[640,640]{1,0:T(8,128)(2,1)}, u32[]{:S(2)}, u32[]{:S(2)}) collective-permute-start(bf16[640,640]{1,0:T(8,128)(2,1)} %get-tuple-element.378), channel_id=1, source_target_pairs={{0,4},{1,5},{2,6},{3,7},{4,8},{5,9},{6,10},{7,11},{16,20},{17,21},... | collective-permute-start | bytes 2457608 | tf_op jit(solution)/shard_map/ppermute | solution.py:195
  64.7 53.3 %collective-permute-start.17 = (bf16[512,640]{1,0:T(8,128)(2,1)}, bf16[512,640]{1,0:T(8,128)(2,1)}, u32[]{:S(2)}, u32[]{:S(2)}) collective-permute-start(bf16[512,640]{1,0:T(8,128)(2,1)} %slice_dynamic-update-slice_fusion), channel_id=1, source_target_pairs={{0,2},{1,3},{2,0},{3,1},{4,6},{5,7},{6,4},{7,5},{8,10},{9,11},{10,... | collective-permute-start | bytes 1966088 | tf_op jit(solution)/shard_map/ppermute | solution.py:199
  82.7 26.9 %collective-permute-start.3 = (bf16[512,640]{1,0:T(8,128)(2,1)}, bf16[512,640]{1,0:T(8,128)(2,1)}, u32[]{:S(2)}, u32[]{:S(2)}) collective-permute-start(bf16[512,640]{1,0:T(8,128)(2,1)} %get-tuple-element.377), channel_id=1, source_target_pairs={{8,4},{9,5},{10,6},{11,7},{4,0},{5,1},{6,2},{7,3},{24,20},{25,21},... | collective-permute-start | bytes 1966088 | tf_op jit(solution)/shard_map/ppermute | solution.py:195
  87.6 27.9 %collective-permute-start.14 = (bf16[640,640]{1,0:T(8,128)(2,1)}, bf16[640,640]{1,0:T(8,128)(2,1)S(1)}, u32[]{:S(2)}, u32[]{:S(2)}) collective-permute-start(bf16[640,640]{1,0:T(8,128)(2,1)} %copy-done.23), channel_id=1, source_target_pairs={{0,4},{1,5},{2,6},{3,7},{4,8},{5,9},{6,10},{7,11},{8,12},{9,13},{1... | collective-permute-start | bytes 2457608 | tf_op jit(solution)/shard_map/ppermute | solution.py:195
  93.3 26.3 %collective-permute-start.18 = (bf16[512,640]{1,0:T(8,128)(2,1)}, bf16[512,640]{1,0:T(8,128)(2,1)}, u32[]{:S(2)}, u32[]{:S(2)}) collective-permute-start(bf16[512,640]{1,0:T(8,128)(2,1)} %broadcast_select_fusion), channel_id=1, source_target_pairs={{0,2},{1,3},{2,0},{3,1},{4,6},{5,7},{6,4},{7,5},{8,10},{9,11},{10,... | collective-permute-start | bytes 1966088 | tf_op jit(solution)/shard_map/ppermute | solution.py:199
  96.8 35.8 %collective-permute-start.10 = (bf16[512,640]{1,0:T(8,128)(2,1)}, bf16[512,640]{1,0:T(8,128)(2,1)}, u32[]{:S(2)}, u32[]{:S(2)}) collective-permute-start(bf16[512,640]{1,0:T(8,128)(2,1)} %collective-permute-done.9), channel_id=1, source_target_pairs={{8,4},{9,5},{10,6},{11,7},{24,20},{25,21},{26,22},{27,23}} | collective-permute-start | bytes 1966088 | tf_op jit(solution)/shard_map/ppermute | solution.py:195
  109.6 26.4 %collective-permute-start.6 = (bf16[544,640]{1,0:T(8,128)(2,1)}, bf16[544,640]{1,0:T(8,128)(2,1)}, u32[]{:S(2)}, u32[]{:S(2)}) collective-permute-start(bf16[544,640]{1,0:T(8,128)(2,1)} %get-tuple-element.379), channel_id=1, source_target_pairs={{4,8},{5,9},{6,10},{7,11},{8,12},{9,13},{10,14},{11,15},{20,24},{2... | collective-permute-start | bytes 2088968 | tf_op jit(solution)/shard_map/ppermute | solution.py:195
  115.5 27.0 %collective-permute-start.19 = (bf16[512,640]{1,0:T(8,128)(2,1)}, bf16[512,640]{1,0:T(8,128)(2,1)}, u32[]{:S(2)}, u32[]{:S(2)}) collective-permute-start(bf16[512,640]{1,0:T(8,128)(2,1)} %get-tuple-element.388), channel_id=1, source_target_pairs={{0,2},{1,3},{2,0},{3,1},{4,6},{5,7},{6,4},{7,5},{8,10},{9,11},{10,... | collective-permute-start | bytes 1966088 | tf_op jit(solution)/shard_map/ppermute | solution.py:199
  118.0 27.9 %collective-permute-start.20 = (bf16[512,640]{1,0:T(8,128)(2,1)}, bf16[512,640]{1,0:T(8,128)(2,1)}, u32[]{:S(2)}, u32[]{:S(2)}) collective-permute-start(bf16[512,640]{1,0:T(8,128)(2,1)} %get-tuple-element.389), channel_id=1, source_target_pairs={{0,2},{1,3},{2,0},{3,1},{4,6},{5,7},{6,4},{7,5},{8,10},{9,11},{10,... | collective-permute-start | bytes 1966088 | tf_op jit(solution)/shard_map/ppermute | solution.py:199
  128.5 23.8 %collective-permute-start.15 = (bf16[544,640]{1,0:T(8,128)(2,1)}, bf16[544,640]{1,0:T(8,128)(2,1)}, u32[]{:S(2)}, u32[]{:S(2)}) collective-permute-start(bf16[544,640]{1,0:T(8,128)(2,1)} %get-tuple-element.385), channel_id=1, source_target_pairs={{4,8},{5,9},{6,10},{7,11},{8,12},{9,13},{10,14},{11,15},{20,24},{2... | collective-permute-start | bytes 2088968 | tf_op jit(solution)/shard_map/ppermute | solution.py:195
  132.6 19.7 %collective-permute-start.11 = (bf16[512,640]{1,0:T(8,128)(2,1)}, bf16[512,640]{1,0:T(8,128)(2,1)}, u32[]{:S(2)}, u32[]{:S(2)}) collective-permute-start(bf16[512,640]{1,0:T(8,128)(2,1)} %collective-permute-done.10), channel_id=1, source_target_pairs={{4,0},{5,1},{6,2},{7,3},{20,16},{21,17},{22,18},{23,19}} | collective-permute-start | bytes 1966088 | tf_op jit(solution)/shard_map/ppermute | solution.py:195
  136.0 68.7 %collective-permute-start.22 = (bf16[512,640]{1,0:T(8,128)(2,1)}, bf16[512,640]{1,0:T(8,128)(2,1)S(1)}, u32[]{:S(2)}, u32[]{:S(2)}) collective-permute-start(bf16[512,640]{1,0:T(8,128)(2,1)} %bitcast.27), channel_id=1, source_target_pairs={{0,1},{1,0},{2,3},{3,2},{4,5},{5,4},{6,7},{7,6},{8,9},{9,8},{10,11... | collective-permute-start | bytes 1966088 | tf_op jit(solution)/shard_map/ppermute | solution.py:199
  142.5 62.2 %collective-permute-start.21 = (bf16[512,640]{1,0:T(8,128)(2,1)}, bf16[512,640]{1,0:T(8,128)(2,1)}, u32[]{:S(2)}, u32[]{:S(2)}) collective-permute-start(bf16[512,640]{1,0:T(8,128)(2,1)} %bitcast.85), channel_id=1, source_target_pairs={{0,1},{1,0},{2,3},{3,2},{4,5},{5,4},{6,7},{7,6},{8,9},{9,8},{10,11... | collective-permute-start | bytes 1966088 | tf_op jit(solution)/shard_map/ppermute | solution.py:199
  145.9 25.8 %collective-permute-start.7 = (bf16[512,640]{1,0:T(8,128)(2,1)}, bf16[512,640]{1,0:T(8,128)(2,1)}, u32[]{:S(2)}, u32[]{:S(2)}) collective-permute-start(bf16[512,640]{1,0:T(8,128)(2,1)} %get-tuple-element.380), channel_id=1, source_target_pairs={{8,12},{9,13},{10,14},{11,15},{4,0},{5,1},{6,2},{7,3},{24,28},{25,... | collective-permute-start | bytes 1966088 | tf_op jit(solution)/shard_map/ppermute | solution.py:195
  152.3 52.4 %collective-permute-start.24 = (bf16[512,640]{1,0:T(8,128)(2,1)}, bf16[512,640]{1,0:T(8,128)(2,1)}, u32[]{:S(2)}, u32[]{:S(2)}) collective-permute-start(bf16[512,640]{1,0:T(8,128)(2,1)} %bitcast.33), channel_id=1, source_target_pairs={{0,1},{1,0},{2,3},{3,2},{4,5},{5,4},{6,7},{7,6},{8,9},{9,8},{10,11... | collective-permute-start | bytes 1966088 | tf_op jit(solution)/shard_map/ppermute | solution.py:199
  152.3 52.4 %collective-permute-start.23 = (bf16[512,640]{1,0:T(8,128)(2,1)}, bf16[512,640]{1,0:T(8,128)(2,1)}, u32[]{:S(2)}, u32[]{:S(2)}) collective-permute-start(bf16[512,640]{1,0:T(8,128)(2,1)} %bitcast.30), channel_id=1, source_target_pairs={{0,1},{1,0},{2,3},{3,2},{4,5},{5,4},{6,7},{7,6},{8,9},{9,8},{10,11... | collective-permute-start | bytes 1966088 | tf_op jit(solution)/shard_map/ppermute | solution.py:199
  (25 other events, 147.2 us)
